TPU v7x, 128 devices: a whole 4x4x4 slice. The times are simulated.
128 devices in a mesh: segment: 2 (over y_hi), expert: 64 (over z, y_lo, x, core).
Axes of the slice: x: 4, y: 4 (y_hi: 2, y_lo: 2; y = y_hi * 2 + y_lo), z: 4, core: 2. Of those that a mesh axis runs over, the one named last changes fastest.
Arguments:
- forward_inputs: bfloat16 [2, 8192, 2048], P('segment', 'expert'), may hold values from -6 to 6
- backward_inputs: bfloat16 [2, 8192, 2048], P('segment', 'expert'), may hold values from -6 to 6
- backward_cotangents: bfloat16 [2, 8192, 2048], P('segment', 'expert'), may hold values from -6 to 6
- routes: int32 [2, 2, 8192, 8], P(None, 'segment', 'expert'), may hold values from 0 to 63, all different within a row; in each aligned block of 128 rows (0 to 127, 128 to 255, ..., all dimensions but the last counted through in order) at most 17 rows name the same one
- route_weights: float32 [2, 2, 8192, 8], P(None, 'segment', 'expert'), may hold values from 0.05 to 0.5
- w_gate: bfloat16 [2, 64, 2048, 768], P('segment', 'expert'), may hold values from -0.125 to 0.125
- w_up: bfloat16 [2, 64, 2048, 768], P('segment', 'expert'), may hold values from -0.125 to 0.125
- w_down: bfloat16 [2, 64, 768, 2048], P('segment', 'expert'), may hold values from -0.21875 to 0.21875
Outputs:
- finished: bfloat16 [2, 8192, 2048], P('segment', 'expert')
- handed: bfloat16 [2, 8192, 2048], P('segment', 'expert')
Inputs may be any that keep to these rules, and one draw needn't show every extreme that they name: `routes`: within the rows of one device (aligned blocks of 128 tokens, for each pass and section) no expert is named by more than 17 (token, pick) pairs, a bound that some block reaches; the 8 experts of a token differ.
All inputs are finite; a program needn't handle non-finite values.
Results may differ from a plain program's by a relative error of at most 0.0047.
Values may be sent and summed in bfloat16 or wider, within the bound.
A program may use at most 128 MiB of HBM per device.

v0:
```python
import jax
import jax.numpy as jnp
from jax import lax
from jax.sharding import PartitionSpec as P


def from_partner(value, axis, stride):
    mask = 2**stride
    pairs = [(source, source ^ mask) for source in range(lax.axis_size(axis))]
    return lax.ppermute(value, axis, pairs)


def dot_transposed(left, right):
    return lax.dot_general(
        left, right, (((1,), (1,)), ((), ())), preferred_element_type=jnp.float32
    )


def slot_plan(route_block, expert_count, capacity):
    token_count = route_block.shape[0]
    expert_ids = jnp.arange(expert_count, dtype=jnp.int32)
    pick_match = route_block[:, :, None] == expert_ids[None, None, :]
    per_token = jnp.sum(pick_match.astype(jnp.float32), axis=1).astype(jnp.bfloat16)
    row_ids = jnp.arange(token_count, dtype=jnp.int32)
    earlier = (row_ids[:, None] > row_ids[None, :]).astype(jnp.bfloat16)
    prior = jnp.dot(earlier, per_token, preferred_element_type=jnp.float32)
    placed = jnp.sum(jnp.where(pick_match, prior[:, None, :], 0.0), axis=2).astype(jnp.int32)
    targets = route_block * capacity + placed
    slot_ids = jnp.arange(expert_count * capacity, dtype=jnp.int32)
    dispatch = jnp.sum(
        (targets[None, :, :] == slot_ids[:, None, None]).astype(jnp.float32), axis=2
    ).astype(jnp.bfloat16)
    return (targets, dispatch)


def pack_rows(row_block, dispatch):
    return jnp.dot(dispatch, row_block, preferred_element_type=jnp.float32).astype(jnp.bfloat16)


def gate_combine(results, targets, weight_block):
    slot_ids = jnp.arange(results.shape[0], dtype=jnp.int32)
    combine = jnp.sum(
        jnp.where(targets[:, :, None] == slot_ids[None, None, :], weight_block[:, :, None], 0.0),
        axis=1,
    )
    return jnp.dot(
        combine,
        results.astype(jnp.float32),
        precision=lax.Precision.HIGHEST,
        preferred_element_type=jnp.float32,
    )


def expert_forward(row_block, gate_w, up_w, down_w):
    gate_pre = jnp.dot(row_block, gate_w, preferred_element_type=jnp.float32)
    up_pre = jnp.dot(row_block, up_w, preferred_element_type=jnp.float32)
    hidden = (jax.nn.silu(gate_pre) * up_pre).astype(jnp.bfloat16)
    return jnp.dot(hidden, down_w, preferred_element_type=jnp.float32).astype(jnp.bfloat16)


def expert_backward(row_block, cotangent, gate_w, up_w, down_w):
    gate_pre = jnp.dot(row_block, gate_w, preferred_element_type=jnp.float32)
    up_pre = jnp.dot(row_block, up_w, preferred_element_type=jnp.float32)
    back_hidden = dot_transposed(cotangent, down_w)
    sigmoid_gate = jax.nn.sigmoid(gate_pre)
    d_gate = (back_hidden * up_pre * sigmoid_gate * (1.0 + gate_pre * (1.0 - sigmoid_gate))).astype(
        jnp.bfloat16
    )
    d_up = (back_hidden * gate_pre * sigmoid_gate).astype(jnp.bfloat16)
    return (dot_transposed(d_gate, gate_w) + dot_transposed(d_up, up_w)).astype(jnp.bfloat16)


def per_device(
    forward_inputs,
    backward_inputs,
    backward_cotangents,
    routes,
    route_weights,
    w_gate,
    w_up,
    w_down,
):
    segment_index = lax.axis_index("segment")
    expert_count = lax.axis_size("expert")
    forward_rows = forward_inputs[0]
    backward_rows = backward_inputs[0]
    cotangent = backward_cotangents[0]
    token_count, width = forward_rows.shape
    top_count = routes.shape[-1]
    capacity = token_count * top_count * 17 // (16 * expert_count)
    gate_w = w_gate[0, 0]
    up_w = w_up[0, 0]
    down_w = w_down[0, 0]
    forward_targets, forward_dispatch_table = slot_plan(routes[0, 0], expert_count, capacity)
    backward_targets, backward_dispatch_table = slot_plan(routes[1, 0], expert_count, capacity)
    forward_packed = pack_rows(forward_rows, forward_dispatch_table).reshape(
        expert_count, capacity, width
    )
    backward_packed = pack_rows(backward_rows, backward_dispatch_table).reshape(
        expert_count, capacity, width
    )
    cot_packed = pack_rows(cotangent, backward_dispatch_table).reshape(
        expert_count, capacity, width
    )
    received = lax.all_to_all(forward_packed, "expert", split_axis=0, concat_axis=0, tiled=True)
    result_rows = expert_forward(received.reshape(-1, width), gate_w, up_w, down_w).reshape(
        received.shape
    )
    forward_back = lax.all_to_all(result_rows, "expert", split_axis=0, concat_axis=0, tiled=True)
    received = (
        lax.all_to_all(backward_packed, "expert", split_axis=0, concat_axis=0, tiled=True),
        lax.all_to_all(cot_packed, "expert", split_axis=0, concat_axis=0, tiled=True),
    )
    result_rows = expert_backward(
        received[0].reshape(-1, width), received[1].reshape(-1, width), gate_w, up_w, down_w
    ).reshape(received[0].shape)
    backward_back = lax.all_to_all(result_rows, "expert", split_axis=0, concat_axis=0, tiled=True)
    forward_mixed = forward_rows.astype(jnp.float32) + gate_combine(
        forward_back.reshape(-1, width), forward_targets, route_weights[0, 0]
    )
    backward_mixed = cotangent.astype(jnp.float32) + gate_combine(
        backward_back.reshape(-1, width), backward_targets, route_weights[1, 0]
    )
    forward_out = forward_mixed.astype(jnp.bfloat16)
    backward_out = backward_mixed.astype(jnp.bfloat16)
    first_segment = segment_index == 0
    finished = jnp.where(first_segment, backward_out, forward_out)
    handed = from_partner(jnp.where(first_segment, forward_out, backward_out), "segment", 0)
    return (finished[None], handed[None])


def solution(mesh):
    placed = (
        P("segment", "expert", None),
        P("segment", "expert", None),
        P("segment", "expert", None),
        P(None, "segment", "expert", None),
        P(None, "segment", "expert", None),
        P("segment", "expert", None, None),
        P("segment", "expert", None, None),
        P("segment", "expert", None, None),
    )
    return jax.shard_map(
        per_device,
        mesh=mesh,
        in_specs=placed,
        out_specs=(P("segment", "expert", None), P("segment", "expert", None)),
        check_vma=False,
    )
```

profile of v0, /device:TPU:1, one launch (start us, length us, event | category | flops | bytes accessed | tf_op | source)
XLA Modules:
  0.0 484.6 jit_solution(9074038446446728767)
XLA Ops:
  13.7 7.6 %reshape.78 = bf16[64,17,2048]{2,1,0:T(8,128)(2,1)} reshape(bf16[1088,2048]{1,0:T(8,128)(2,1)} %convolution_convert_fusion.2) | data formatting | bytes 8912896 | tf_op jit(solution)/shard_map/reshape | solution.py:99
  21.3 11.0 %all-to-all-start.1 = ((bf16[64,17,2048]{2,1,0:T(8,128)(2,1)}), bf16[64,17,2048]{2,1,0:T(8,128)(2,1)}, u32[]{:S(2)}, u32[]{:S(2)}) async-start(bf16[64,17,2048]{2,1,0:T(8,128)(2,1)} %reshape.78), calls=%async_computation.1 | async-start | bytes 12582912 | tf_op jit(solution)/shard_map/all_to_all | solution.py:111
  36.7 7.6 %reshape.76 = bf16[64,17,2048]{2,1,0:T(8,128)(2,1)} reshape(bf16[1088,2048]{1,0:T(8,128)(2,1)} %convolution_convert_fusion.3) | data formatting | bytes 8912896 | tf_op jit(solution)/shard_map/reshape | solution.py:102
  44.3 65.0 %all-to-all-done.1 = bf16[64,17,2048]{2,1,0:T(8,128)(2,1)} async-done(((bf16[64,17,2048]{2,1,0:T(8,128)(2,1)}), bf16[64,17,2048]{2,1,0:T(8,128)(2,1)}, u32[]{:S(2)}, u32[]{:S(2)}) %all-to-all-start.1) | async-done | bytes 4456480 | tf_op jit(solution)/shard_map/all_to_all | solution.py:111
  109.3 9.8 %all-to-all-start = ((bf16[64,17,2048]{2,1,0:T(8,128)(2,1)}), bf16[64,17,2048]{2,1,0:T(8,128)(2,1)}, u32[]{:S(2)}, u32[]{:S(2)}) async-start(bf16[64,17,2048]{2,1,0:T(8,128)(2,1)} %reshape.76), calls=%async_computation | async-start | bytes 12582912 | tf_op jit(solution)/shard_map/all_to_all | solution.py:112
  123.5 7.6 %reshape.82 = bf16[64,17,2048]{2,1,0:T(8,128)(2,1)} reshape(bf16[1088,2048]{1,0:T(8,128)(2,1)} %convolution_convert_fusion.1) | data formatting | bytes 8912896 | tf_op jit(solution)/shard_map/reshape | solution.py:96
  131.0 7.7 %reshape.79 = bf16[1088,2048]{1,0:T(8,128)(2,1)} reshape(bf16[64,17,2048]{2,1,0:T(8,128)(2,1)} %all-to-all-done.1) | data formatting | bytes 8912896 | tf_op jit(solution)/shard_map/reshape | solution.py:115
  138.8 7.6 %fusion.9 = f32[1088,768]{1,0:T(8,128)} fusion(bf16[1088,2048]{1,0:T(8,128)(2,1)} %reshape.79, bf16[1,1,2048,768]{3,2,1,0:T(8,128)(2,1)S(1)} %copy-done), kind=kOutput, calls=%fused_computation.26 | convolution fusion | flops 3422552064 | bytes 10944512 | tf_op jit(solution)/shard_map/dot_general | solution.py:62
  146.4 49.3 %all-to-all-done = bf16[64,17,2048]{2,1,0:T(8,128)(2,1)} async-done(((bf16[64,17,2048]{2,1,0:T(8,128)(2,1)}), bf16[64,17,2048]{2,1,0:T(8,128)(2,1)}, u32[]{:S(2)}, u32[]{:S(2)}) %all-to-all-start) | async-done | bytes 4456480 | tf_op jit(solution)/shard_map/all_to_all | solution.py:112
  195.7 9.6 %all-to-all-start.3 = ((bf16[64,17,2048]{2,1,0:T(8,128)(2,1)}), bf16[64,17,2048]{2,1,0:T(8,128)(2,1)}, u32[]{:S(2)}, u32[]{:S(2)}) async-start(bf16[64,17,2048]{2,1,0:T(8,128)(2,1)} %reshape.82), calls=%async_computation.3 | async-start | bytes 12582912 | tf_op jit(solution)/shard_map/all_to_all | solution.py:105
  205.3 7.8 %reshape.77 = bf16[1088,2048]{1,0:T(8,128)(2,1)} reshape(bf16[64,17,2048]{2,1,0:T(8,128)(2,1)} %all-to-all-done) | data formatting | bytes 8912896 | tf_op jit(solution)/shard_map/reshape | solution.py:115
  213.1 6.6 %fusion.15 = f32[1088,768]{1,0:T(8,128)S(1)} fusion(bf16[1088,2048]{1,0:T(8,128)(2,1)} %reshape.77, bf16[1,1,768,2048]{3,2,1,0:T(8,128)(2,1)} %param.15), kind=kOutput, calls=%fused_computation.32 | convolution fusion | flops 3422552064 | bytes 10944512 | tf_op jit(solution)/shard_map/dot_general | solution.py:14
  228.0 8.6 %fusion = bf16[1088,2048]{1,0:T(8,128)(2,1)} fusion(f32[1088,2048]{1,0:T(8,128)S(1)} %fusion.7, bf16[1,1,2048,768]{3,2,1,0:T(8,128)(2,1)S(1)} %copy-done.4, f32[1088,768]{1,0:T(8,128)} %copy-done.8, f32[1088,768]{1,0:T(8,128)} %fusion.9), kind=kOutput, calls=%fused_computation.1 | convolution fusion | flops 3432022016 | bytes 23199744 | tf_op jit(solution)/shard_map/dot_general | solution.py:14
  236.6 7.6 %reshape.80 = bf16[64,17,2048]{2,1,0:T(8,128)(2,1)} reshape(bf16[1088,2048]{1,0:T(8,128)(2,1)} %fusion) | data formatting | bytes 8912896 | tf_op jit(solution)/shard_map/reshape | solution.py:116
  244.2 37.8 %all-to-all-done.3 = bf16[64,17,2048]{2,1,0:T(8,128)(2,1)} async-done(((bf16[64,17,2048]{2,1,0:T(8,128)(2,1)}), bf16[64,17,2048]{2,1,0:T(8,128)(2,1)}, u32[]{:S(2)}, u32[]{:S(2)}) %all-to-all-start.3) | async-done | bytes 4456480 | tf_op jit(solution)/shard_map/all_to_all | solution.py:105
  282.0 9.6 %all-to-all-start.2 = ((bf16[64,17,2048]{2,1,0:T(8,128)(2,1)}), bf16[64,17,2048]{2,1,0:T(8,128)(2,1)}, u32[]{:S(2)}, u32[]{:S(2)}) async-start(bf16[64,17,2048]{2,1,0:T(8,128)(2,1)} %reshape.80), calls=%async_computation.2 | async-start | bytes 12582912 | tf_op jit(solution)/shard_map/all_to_all | solution.py:117
  291.6 7.7 %reshape.83 = bf16[1088,2048]{1,0:T(8,128)(2,1)} reshape(bf16[64,17,2048]{2,1,0:T(8,128)(2,1)} %all-to-all-done.3) | data formatting | bytes 8912896 | tf_op jit(solution)/shard_map/reshape | solution.py:106
  314.4 7.7 %reshape.84 = bf16[64,17,2048]{2,1,0:T(8,128)(2,1)} reshape(bf16[1088,2048]{1,0:T(8,128)(2,1)} %convolution_convert_fusion) | data formatting | bytes 8912896 | tf_op jit(solution)/shard_map/reshape | solution.py:106
  322.1 46.2 %all-to-all-done.2 = bf16[64,17,2048]{2,1,0:T(8,128)(2,1)} async-done(((bf16[64,17,2048]{2,1,0:T(8,128)(2,1)}), bf16[64,17,2048]{2,1,0:T(8,128)(2,1)}, u32[]{:S(2)}, u32[]{:S(2)}) %all-to-all-start.2) | async-done | bytes 4456480 | tf_op jit(solution)/shard_map/all_to_all | solution.py:117
  368.3 9.7 %all-to-all-start.4 = ((bf16[64,17,2048]{2,1,0:T(8,128)(2,1)}), bf16[64,17,2048]{2,1,0:T(8,128)(2,1)}, u32[]{:S(2)}, u32[]{:S(2)}) async-start(bf16[64,17,2048]{2,1,0:T(8,128)(2,1)} %reshape.84), calls=%async_computation.4 | async-start | bytes 12582912 | tf_op jit(solution)/shard_map/all_to_all | solution.py:109
  380.1 7.7 %reshape.81 = bf16[1088,2048]{1,0:T(8,128)(2,1)} reshape(bf16[64,17,2048]{2,1,0:T(8,128)(2,1)} %all-to-all-done.2) | data formatting | bytes 8912896 | tf_op jit(solution)/shard_map/reshape | solution.py:122
  393.5 61.2 %all-to-all-done.4 = bf16[64,17,2048]{2,1,0:T(8,128)(2,1)} async-done(((bf16[64,17,2048]{2,1,0:T(8,128)(2,1)}), bf16[64,17,2048]{2,1,0:T(8,128)(2,1)}, u32[]{:S(2)}, u32[]{:S(2)}) %all-to-all-start.4) | async-done | bytes 4456480 | tf_op jit(solution)/shard_map/all_to_all | solution.py:109
  454.6 7.7 %reshape.85 = bf16[1088,2048]{1,0:T(8,128)(2,1)} reshape(bf16[64,17,2048]{2,1,0:T(8,128)(2,1)} %all-to-all-done.4) | data formatting | bytes 8912896 | tf_op jit(solution)/shard_map/reshape | solution.py:119
  470.9 12.6 %collective-permute-done = bf16[128,2048]{1,0:T(8,128)(2,1)S(1)} collective-permute-done((bf16[128,2048]{1,0:T(8,128)(2,1)S(1)}, bf16[128,2048]{1,0:T(8,128)(2,1)S(1)}, u32[]{:S(2)}, u32[]{:S(2)}) %collective-permute-start) | collective-permute-done | bytes 524320 | tf_op jit(solution)/shard_map/ppermute | solution.py:10
  (46 shorter events, 62.0 us)
Async XLA Ops:
  0.6 138.2 %copy-start = (bf16[1,1,2048,768]{3,2,1,0:T(8,128)(2,1)S(1)}, bf16[1,1,2048,768]{3,2,1,0:T(8,128)(2,1)}, u32[]{:S(2)}) copy-start(bf16[1,1,2048,768]{3,2,1,0:T(8,128)(2,1)} %param.13) | copy-start | bytes 9437188
  21.3 88.0 %all-to-all-start.1 = ((bf16[64,17,2048]{2,1,0:T(8,128)(2,1)}), bf16[64,17,2048]{2,1,0:T(8,128)(2,1)}, u32[]{:S(2)}, u32[]{:S(2)}) async-start(bf16[64,17,2048]{2,1,0:T(8,128)(2,1)} %reshape.78), calls=%async_computation.1 | async-start | bytes 12582912 | tf_op jit(solution)/shard_map/all_to_all | solution.py:111
  44.3 74.8 %copy-start.2 = (bf16[1088,128]{1,0:T(8,128)(2,1)S(1)}, bf16[1088,128]{1,0:T(8,128)(2,1)}, u32[]{:S(2)}) copy-start(bf16[1088,128]{1,0:T(8,128)(2,1)} %get-tuple-element.12) | copy-start | bytes 835588
  109.3 86.4 %all-to-all-start = ((bf16[64,17,2048]{2,1,0:T(8,128)(2,1)}), bf16[64,17,2048]{2,1,0:T(8,128)(2,1)}, u32[]{:S(2)}, u32[]{:S(2)}) async-start(bf16[64,17,2048]{2,1,0:T(8,128)(2,1)} %reshape.76), calls=%async_computation | async-start | bytes 12582912 | tf_op jit(solution)/shard_map/all_to_all | solution.py:112
  195.7 86.3 %all-to-all-start.3 = ((bf16[64,17,2048]{2,1,0:T(8,128)(2,1)}), bf16[64,17,2048]{2,1,0:T(8,128)(2,1)}, u32[]{:S(2)}, u32[]{:S(2)}) async-start(bf16[64,17,2048]{2,1,0:T(8,128)(2,1)} %reshape.82), calls=%async_computation.3 | async-start | bytes 12582912 | tf_op jit(solution)/shard_map/all_to_all | solution.py:105
  205.3 14.4 %slice-start = ((s8[4456448]{0:T(1024)(128)(4,1)}), s8[262144]{0:T(1024)(128)(4,1)S(1)}, s32[]{:S(2)}) async-start(s8[4456448]{0:T(1024)(128)(4,1)} %bitcast.63), calls=%async_computation.5 | async-start | bytes 524288
  213.1 6.6 %slice-start.1 = ((s8[4456448]{0:T(1024)(128)(4,1)}), s8[4194304]{0:T(1024)(128)(4,1)S(1)}, s32[]{:S(2)}) async-start(s8[4456448]{0:T(1024)(128)(4,1)} %bitcast.63), calls=%async_computation.6 | async-start | bytes 8388608
  213.1 6.6 %copy-start.4 = (bf16[1,1,2048,768]{3,2,1,0:T(8,128)(2,1)S(1)}, bf16[1,1,2048,768]{3,2,1,0:T(8,128)(2,1)}, u32[]{:S(2)}) copy-start(bf16[1,1,2048,768]{3,2,1,0:T(8,128)(2,1)} %param.14) | copy-start | bytes 9437188
  213.1 6.7 %copy-start.7 = (f32[1088,768]{1,0:T(8,128)S(1)}, f32[1088,768]{1,0:T(8,128)}, u32[]{:S(2)}) copy-start(f32[1088,768]{1,0:T(8,128)} %fusion.9) | copy-start | bytes 10027012
  219.8 4.5 copy-start.8
  282.0 86.3 %all-to-all-start.2 = ((bf16[64,17,2048]{2,1,0:T(8,128)(2,1)}), bf16[64,17,2048]{2,1,0:T(8,128)(2,1)}, u32[]{:S(2)}, u32[]{:S(2)}) async-start(bf16[64,17,2048]{2,1,0:T(8,128)(2,1)} %reshape.80), calls=%async_computation.2 | async-start | bytes 12582912 | tf_op jit(solution)/shard_map/all_to_all | solution.py:117
  299.4 5.7 %copy-start.1 = (bf16[1088,2048]{1,0:T(8,128)(2,1)S(1)}, bf16[1088,2048]{1,0:T(8,128)(2,1)}, u32[]{:S(2)}) copy-start(bf16[1088,2048]{1,0:T(8,128)(2,1)} %reshape.83) | copy-start | bytes 13369348
  299.4 5.8 %copy-start.5 = (bf16[1,1,2048,768]{3,2,1,0:T(8,128)(2,1)S(1)}, bf16[1,1,2048,768]{3,2,1,0:T(8,128)(2,1)}, u32[]{:S(2)}) copy-start(bf16[1,1,2048,768]{3,2,1,0:T(8,128)(2,1)} %param.14) | copy-start | bytes 9437188
  305.2 3.9 copy-start.6
  322.1 55.9 %copy-start.3 = (f32[2,1,128,8]{2,3,1,0:T(8,128)S(1)}, f32[2,1,128,8]{2,3,1,0:T(8,128)}, u32[]{:S(2)}) copy-start(f32[2,1,128,8]{2,3,1,0:T(8,128)} %param.12) | copy-start | bytes 24580
  368.3 86.3 %all-to-all-start.4 = ((bf16[64,17,2048]{2,1,0:T(8,128)(2,1)}), bf16[64,17,2048]{2,1,0:T(8,128)(2,1)}, u32[]{:S(2)}, u32[]{:S(2)}) async-start(bf16[64,17,2048]{2,1,0:T(8,128)(2,1)} %reshape.84), calls=%async_computation.4 | async-start | bytes 12582912 | tf_op jit(solution)/shard_map/all_to_all | solution.py:109
  468.3 15.3 %collective-permute-start = (bf16[128,2048]{1,0:T(8,128)(2,1)S(1)}, bf16[128,2048]{1,0:T(8,128)(2,1)S(1)}, u32[]{:S(2)}, u32[]{:S(2)}) collective-permute-start(bf16[128,2048]{1,0:T(8,128)(2,1)S(1)} %get-tuple-element.2), channel_id=1, source_target_pairs={{0,64},{64,0},{1,65},{65,1},{2,66},{66,2},{3,67},{67,3},{4,68},{68... | collective-permute-start | bytes 1572872 | tf_op jit(solution)/shard_map/ppermute | solution.py:10
where the time goes:
time: 493 us; the launch traced here: 485 us
  waiting for transfers between devices  272 us (55%)
  local copies, waits for them, and re-layouts  78.5 us (16%)
  matrix products  70.9 us (14%)
  starting transfers between devices  52.3 us (11%)
  other arithmetic  9.51 us (2%)
    all_to_all x2, waiting for transfers between devices, per_device(): lax.all_to_all(result_rows, 'expert', split_axis=0, concat_axis=0, tiled=...  107 us
    all_to_all x1, waiting for transfers between devices, per_device(): lax.all_to_all(backward_packed, 'expert', split_axis=0, concat_axis=0, ti...  65 us
    all_to_all x1, waiting for transfers between devices, per_device(): lax.all_to_all(cot_packed, 'expert', split_axis=0, concat_axis=0, tiled=T...  49.3 us
    all_to_all x1, waiting for transfers between devices, per_device(): lax.all_to_all(forward_packed, 'expert', split_axis=0, concat_axis=0, til...  37.8 us
    all_to_all x2, starting transfers between devices, per_device(): lax.all_to_all(result_rows, 'expert', split_axis=0, concat_axis=0, tiled=...  19.3 us
    dot_general x3, matrix products, dot_transposed(): lax.dot_general(left, right, (((1,), (1,)), ((), ())), preferred_element_...  18.9 us
    dot_general x3, matrix products, pack_rows(): jnp.dot(dispatch, row_block, preferred_element_type=jnp.float32)  13.2 us
    ppermute x1, waiting for transfers between devices, from_partner(): return lax.ppermute(value, axis, pairs)  12.6 us
  transfers between devices with their start and end apart: 6, of which 6 were waited for; matrix products, arithmetic and copies ran while one was open for 26% of the time, Pallas kernels for 0%

commit v1 on v0

v1 whole, which is shorter than its diff:
```python
import functools

import jax
import jax.numpy as jnp
from jax import lax
from jax.experimental import pallas as pl
from jax.experimental.pallas import tpu as pltpu
from jax.sharding import PartitionSpec as P

MESH = pl.DeviceIdType.MESH
F32 = jnp.float32
BF16 = jnp.bfloat16

TOK = 128
CAP = 17
SRC = 8
DST = 8
BLK = 144
TILES = BLK // 16
FAR = (2, 1, 3)
DIRECT = (96, 32, 32)
REDUCE = (32, 96)


def dot(left, right):
    return jnp.dot(left, right, preferred_element_type=F32)


def dot_nt(left, right):
    return lax.dot_general(left, right, (((1,), (1,)), ((), ())), preferred_element_type=F32)


def dot_tn(left, right):
    return lax.dot_general(left, right, (((0,), (0,)), ((), ())), preferred_element_type=F32)


def kernel(
    xf, xb, xc, routes, weights, wg_hbm, wu_hbm, wd_hbm,
    out_f, out_b, gathered,
    town, table, gt, packed, recv, back, c_left, c_right, f_y, f_a, acc, hid, wg, wu, wd,
    w_sem, fetch_sem, loc_sem, oloc_sem,
    t_s, t_r, g1_s, g1_r, g2_s, g2_r, g3_s, g3_r, g4_s, g4_r, a_s, a_r, o_s, o_r,
    c1_s, c1_r, c2_s, c2_r, c3_s, c3_r, c4_s, c4_r,
):
    seg = lax.axis_index("segment")
    me = lax.axis_index("expert")
    z, y, x, c = me // 16, (me // 8) % 2, (me // 2) % 4, me % 2
    a = z * (1 - c) + x * c
    b = x * (1 - c) + z * c
    inputs = (xf, xb, xc)

    def device(aa, yy, bb, cc):
        zz = aa * (1 - c) + bb * c
        xx = bb * (1 - c) + aa * c
        return (seg, ((zz * 2 + yy) * 4 + xx) * 2 + cc)

    def at_a(d, dy=0):
        return device((a + d) % 4, (y + dy) % 2, b, c)

    def source(d, dy=0):
        return ((a + d + 4) % 4) * 2 + (y + dy) % 2

    own = a * 2 + y

    def remote(src, dst, send, rec, to):
        return pltpu.make_async_remote_copy(
            src_ref=src, dst_ref=dst, send_sem=send, recv_sem=rec, device_id=to, device_id_type=MESH
        )

    loads = [
        pltpu.make_async_copy(src, dst, w_sem.at[i])
        for i, (src, dst) in enumerate(((wg_hbm, wg), (wu_hbm, wu), (wd_hbm, wd)))
    ]

    barrier = pltpu.get_barrier_semaphore()
    partners = [at_a(d, dy) for d in range(4) for dy in range(2) if d or dy]
    partners += [device(a, y, (b + d) % 4, c) for d in (1, 2, 3)]
    partners += [device(a, y, (b + d) % 4, 1 - c) for d in range(4)]
    partners += [device((a + d) % 4, y, b, 1 - c) for d in (1, 2, 3)]
    for to in partners:
        pl.semaphore_signal(barrier, inc=1, device_id=to, device_id_type=MESH)
    pl.semaphore_wait(barrier, len(partners))

    def g1(q):
        return remote(inputs[q], gathered.at[q, own], g1_s.at[q], g1_r.at[q], at_a(0, 1))

    def g2(q, d):
        return remote(inputs[q], gathered.at[q, own], g2_s.at[q, d], g2_r.at[q, d], at_a(d))

    def g3(q, d):
        part = gathered.at[q, source(0, 1), pl.ds(0, DIRECT[q])]
        return remote(part, part, g3_s.at[q, d], g3_r.at[q, d], at_a(d))

    def g4(q, d):
        part = gathered.at[q, source(-d), pl.ds(DIRECT[q], TOK - DIRECT[q])]
        return remote(part, part, g4_s.at[q, d], g4_r.at[q, d], at_a(0, 1))

    def gather_own(q):
        g1(q).start()
        for d in FAR:
            g2(q, d).start()

    def gather_relay(q):
        g1(q).wait_recv()
        for d in FAR:
            g3(q, d).start()
        for d in (1, 3, 2):
            g2(q, d).wait_recv()
            g4(q, d).start()

    def gather_rest(q):
        for d in FAR:
            g3(q, d).wait_recv()
            g4(q, d).wait_recv()

    gather_own(0)
    for load in loads:
        load.start()

    row = lax.broadcasted_iota(jnp.int32, (64, TOK), 0)
    ra, ry, rb, rc = row // 16, (row // 8) % 2, (row // 2) % 4, row % 2
    expert = (
        ((ra * (1 - c) + rb * c) * 2 + ry) * 4 + (rb * (1 - c) + ra * c)
    ) * 2 + rc
    before = (
        lax.broadcasted_iota(jnp.int32, (TOK, TOK), 0)
        < lax.broadcasted_iota(jnp.int32, (TOK, TOK), 1)
    ).astype(F32).astype(BF16)
    for p in range(2):
        named = jnp.zeros((64, TOK), F32)
        weight = jnp.zeros((64, TOK), F32)
        for j in range(8):
            hit = routes[p, j : j + 1, :] == expert
            named = jnp.where(hit, 1.0, named)
            weight = jnp.where(hit, weights[p, j : j + 1, :], weight)
        prior = dot(named.astype(BF16), before)
        place = jnp.where(named > 0.5, prior, -1000.0)
        for g in range(8):
            town[g, 2 * p] = place[8 * g : 8 * g + 8]
            town[g, 2 * p + 1] = weight[8 * g : 8 * g + 8]

    def send_table(d, dy):
        return remote(
            town.at[source(d, dy)], table.at[own], t_s.at[2 * d + dy], t_r.at[2 * d + dy], at_a(d, dy)
        )

    near = [(d, dy) for d in range(4) for dy in range(2) if d or dy]
    for d, dy in near:
        send_table(d, dy).start()
    table[own] = town[own]

    def fetch(q, d, dy):
        s = source(d, dy)
        src = inputs[q] if (d, dy) == (0, 0) else gathered.at[q, s]
        return pltpu.make_async_copy(src, gt.at[s], fetch_sem.at[2 * d + dy])

    slot_row = lax.broadcasted_iota(jnp.int32, (DST, 16, TOK), 1).astype(F32)

    def pack(q, buf):
        def step(i, carry):
            s0 = jnp.clip(i - 1, 0, SRC - 2)
            parts = []
            for o in range(2):
                place = table[s0 + o, 2 * min(q, 1)]
                shift = (CAP * (s0 + o) - 16 * i).astype(F32)
                parts.append(
                    jnp.where(place[:, None, :] + shift == slot_row, 1.0, 0.0).reshape(DST * 16, TOK)
                )
            pick = jnp.concatenate(parts, axis=1).astype(BF16)
            rows = gt[pl.ds(s0, 2)].reshape(2 * TOK, 2048)
            made = dot(pick, rows).astype(BF16).reshape(DST, 16, 2048)
            packed[buf, :, pl.ds(pl.multiple_of(16 * i, 16), 16), :] = made
            return carry

        lax.fori_loop(0, TILES, step, 0)

    near_b = [(d, dc) for d in (2, 1, 3, 0) for dc in range(2) if d or dc]

    def scatter(q, buf, d, dc):
        bb, cc = (b + d) % 4, (c + dc) % 2
        return remote(
            packed.at[buf, bb * 2 + cc], recv.at[q, 2 * d + dc], a_s.at[q, 2 * d + dc],
            a_r.at[q, 2 * d + dc], device(a, y, bb, cc),
        )

    def scatter_own(q, buf):
        return pltpu.make_async_copy(packed.at[buf, b * 2 + c], recv.at[q, 0], loc_sem.at[q])

    def pack_and_send(q, buf):
        for d in range(4):
            for dy in range(2):
                fetch(q, d, dy).start()
        for d in range(4):
            for dy in range(2):
                fetch(q, d, dy).wait()
        pack(q, buf)
        for d, dc in near_b:
            scatter(q, buf, d, dc).start()
        scatter_own(q, buf).start()

    def scatter_wait(q, buf, k):
        @pl.when(k == 0)
        def _():
            scatter_own(q, buf).wait()

        @pl.when(k > 0)
        def _():
            scatter(q, buf, k, 0).wait_recv()

        scatter(q, buf, k, 1).wait_recv()

    def result_same(q, p, k):
        return remote(
            recv.at[q, 2 * k], back.at[p, b * 2 + c], o_s.at[p, 2 * k], o_r.at[p, 2 * k],
            device(a, y, (b - k + 4) % 4, c),
        )

    def result_other(q, p, k):
        return remote(
            recv.at[q, 2 * k + 1], back.at[p, a * 2 + c], o_s.at[p, 2 * k + 1], o_r.at[p, 2 * k + 1],
            device((a - k + 4) % 4, y, b, 1 - c),
        )

    def result_own(q, p):
        return pltpu.make_async_copy(recv.at[q, 0], back.at[p, b * 2 + c], oloc_sem.at[p])

    def send_results(q, p, k):
        @pl.when(k == 0)
        def _():
            result_own(q, p).start()

        @pl.when(k > 0)
        def _():
            result_same(q, p, k).start()

        result_other(q, p, k).start()

    def results_wait(q, p):
        result_own(q, p).wait()
        for k in range(4):
            if k:
                result_same(q, p, k).wait_recv()
            result_other(q, p, k).wait_recv()

    def forward_step(k, carry):
        scatter_wait(0, 0, k)
        rows = recv[0, pl.ds(2 * k, 2)].reshape(2 * BLK, 2048)
        for n in range(3):
            cols = slice(256 * n, 256 * n + 256)
            gate = dot(rows, wg[:, cols])
            up = dot(rows, wu[:, cols])
            hid[0, :, cols] = (gate * jax.nn.sigmoid(gate) * up).astype(BF16)
        for n in range(4):
            cols = slice(512 * n, 512 * n + 512)
            recv[0, pl.ds(2 * k, 2), :, cols] = (
                dot(hid[0], wd[:, cols]).astype(BF16).reshape(2, BLK, 512)
            )
        send_results(0, 0, k)
        return carry

    def backward_step(k, carry):
        scatter_wait(1, 1, k)
        scatter_wait(2, 0, k)
        rows = recv[1, pl.ds(2 * k, 2)].reshape(2 * BLK, 2048)
        cot = recv[2, pl.ds(2 * k, 2)].reshape(2 * BLK, 2048)
        for n in range(3):
            cols = slice(256 * n, 256 * n + 256)
            gate = dot(rows, wg[:, cols])
            up = dot(rows, wu[:, cols])
            grad = dot_nt(cot, wd[cols, :])
            sig = jax.nn.sigmoid(gate)
            hid[0, :, cols] = (grad * up * sig * (1.0 + gate * (1.0 - sig))).astype(BF16)
            hid[1, :, cols] = (grad * gate * sig).astype(BF16)
        for n in range(4):
            cols = slice(512 * n, 512 * n + 512)
            recv[1, pl.ds(2 * k, 2), :, cols] = (
                (dot_nt(hid[0], wg[cols, :]) + dot_nt(hid[1], wu[cols, :]))
                .astype(BF16)
                .reshape(2, BLK, 512)
            )
        send_results(1, 1, k)
        return carry

    pair_row = lax.broadcasted_iota(jnp.int32, (DST, 32, TOK), 1).astype(F32)

    def partial(p, d, dy):
        s = source(d, dy)
        place = table[s, 2 * p]
        weight = table[s, 2 * p + 1]
        hit = place[:, None, :] + s.astype(F32) == pair_row
        mix = jnp.where(hit, weight[:, None, :], 0.0).reshape(DST * 32, TOK).astype(BF16)
        rows = back[p, :, pl.ds(pl.multiple_of(16 * s, 16), 32), :].reshape(DST * 32, 2048)
        return dot_tn(mix, rows)

    sums = gt

    def c1(p, d):
        cut = REDUCE[p]
        return remote(
            sums.at[2 * d + 1, pl.ds(0, cut)], c_left.at[p, d - 1, pl.ds(0, cut)],
            c1_s.at[p, d], c1_r.at[p, d], at_a(d),
        )

    def c2(p, d):
        cut = REDUCE[p]
        rest = pl.ds(cut, TOK - cut)
        dst = c_right.at[p, d - 1, rest] if d else f_y.at[p, rest]
        return remote(sums.at[2 * d + 1, rest], dst, c2_s.at[p, d], c2_r.at[p, d], at_a(0, 1))

    def c3(p):
        part = pl.ds(0, REDUCE[p])
        return remote(sums.at[1, part], f_y.at[p, part], c3_s.at[p], c3_r.at[p], at_a(0, 1))

    def c4(p, d):
        return remote(sums.at[2 * d], f_a.at[p, d - 1], c4_s.at[p, d], c4_r.at[p, d], at_a(d))

    def combine_start(p):
        for d in (2, 1, 3):
            sums[2 * d + 1] = partial(p, d, 1).astype(BF16)
            c1(p, d).start()
            c2(p, d).start()
        sums[1] = partial(p, 0, 1).astype(BF16)
        c2(p, 0).start()
        for d in (2, 1, 3):
            sums[2 * d] = partial(p, d, 0).astype(BF16)
        acc[...] = partial(p, 0, 0) + inputs[2 * p][...].astype(F32)

    def combine_middle(p):
        cut = REDUCE[p]
        for d in (2, 1, 3):
            c2(p, d).wait_recv()
            sums[2 * d, cut:, :] = (
                sums[2 * d, cut:, :].astype(F32) + c_right[p, d - 1, cut:, :].astype(F32)
            ).astype(BF16)
            c4(p, d).start()
        for d in (1, 3, 2):
            c1(p, d).wait_recv()
        total = sums[1, :cut, :].astype(F32)
        for d in (1, 2, 3):
            total += c_left[p, d - 1, :cut, :].astype(F32)
        sums[1, :cut, :] = total.astype(BF16)
        c3(p).start()

    def combine_end(p, out):
        for d in (1, 3, 2):
            c4(p, d).wait_recv()
        c2(p, 0).wait_recv()
        c3(p).wait_recv()
        total = acc[...] + f_y[p].astype(F32)
        for d in (1, 2, 3):
            total += f_a[p, d - 1].astype(F32)
        out[...] = total.astype(BF16)

    def combine_sent(p):
        for d in range(4):
            if d:
                c1(p, d).wait_send()
                c4(p, d).wait_send()
            c2(p, d).wait_send()
        c3(p).wait_send()

    gather_relay(0)
    gather_own(1)
    gather_rest(0)
    for d, dy in near:
        send_table(d, dy).wait_recv()
    pack_and_send(0, 0)
    gather_relay(1)
    gather_own(2)
    gather_rest(1)
    pack_and_send(1, 1)
    gather_relay(2)
    for load in loads:
        load.wait()
    lax.fori_loop(0, 4, forward_step, 0)
    gather_rest(2)
    for d, dc in near_b:
        scatter(0, 0, d, dc).wait_send()
    pack_and_send(2, 0)
    results_wait(0, 0)
    combine_start(0)
    lax.fori_loop(0, 4, backward_step, 0)
    combine_middle(0)
    combine_end(0, out_f)
    combine_sent(0)
    results_wait(1, 1)
    combine_start(1)
    combine_middle(1)
    combine_end(1, out_b)
    combine_sent(1)

    for d, dy in near:
        send_table(d, dy).wait_send()
    for q in range(3):
        g1(q).wait_send()
        for d in FAR:
            g2(q, d).wait_send()
            g3(q, d).wait_send()
            g4(q, d).wait_send()
    for d, dc in near_b:
        scatter(1, 1, d, dc).wait_send()
        scatter(2, 0, d, dc).wait_send()
    for q in range(2):
        for k in range(4):
            if k:
                result_same(q, q, k).wait_send()
            result_other(q, q, k).wait_send()


def moe(xf, xb, xc, routes, weights, wg, wu, wd):
    vmem = pl.BlockSpec(memory_space=pltpu.VMEM)
    hbm = pl.BlockSpec(memory_space=pl.ANY)
    dma = pltpu.SemaphoreType.DMA
    block = (TOK, 2048)
    out_f, out_b, _ = pl.pallas_call(
        kernel,
        out_shape=(
            jax.ShapeDtypeStruct(block, BF16),
            jax.ShapeDtypeStruct(block, BF16),
            jax.ShapeDtypeStruct((3, SRC) + block, BF16),
        ),
        in_specs=[vmem] * 5 + [hbm] * 3,
        out_specs=(vmem, vmem, hbm),
        scratch_shapes=[
            pltpu.VMEM((8, 4, 8, TOK), F32),
            pltpu.VMEM((8, 4, 8, TOK), F32),
            pltpu.VMEM((SRC,) + block, BF16),
            pltpu.VMEM((2, DST, BLK, 2048), BF16),
            pltpu.VMEM((3, 8, BLK, 2048), BF16),
            pltpu.VMEM((2, DST, BLK, 2048), BF16),
            pltpu.VMEM((2, 3) + block, BF16),
            pltpu.VMEM((2, 3) + block, BF16),
            pltpu.VMEM((2,) + block, BF16),
            pltpu.VMEM((2, 3) + block, BF16),
            pltpu.VMEM(block, F32),
            pltpu.VMEM((2, 2 * BLK, 768), BF16),
            pltpu.VMEM((2048, 768), BF16),
            pltpu.VMEM((2048, 768), BF16),
            pltpu.VMEM((768, 2048), BF16),
            dma((3,)), dma((8,)), dma((3,)), dma((2,)),
            dma((8,)), dma((8,)),
            dma((3,)), dma((3,)),
            dma((3, 4)), dma((3, 4)),
            dma((3, 4)), dma((3, 4)),
            dma((3, 4)), dma((3, 4)),
            dma((3, 8)), dma((3, 8)),
            dma((2, 8)), dma((2, 8)),
            dma((2, 4)), dma((2, 4)),
            dma((2, 4)), dma((2, 4)),
            dma((2,)), dma((2,)),
            dma((2, 4)), dma((2, 4)),
        ],
        compiler_params=pltpu.CompilerParams(
            collective_id=0, has_side_effects=True, vmem_limit_bytes=63 * 2**20
        ),
    )(xf, xb, xc, routes, weights, wg, wu, wd)
    return out_f, out_b


def per_device(
    forward_inputs,
    backward_inputs,
    backward_cotangents,
    routes,
    route_weights,
    w_gate,
    w_up,
    w_down,
):
    forward_out, backward_out = moe(
        forward_inputs[0],
        backward_inputs[0],
        backward_cotangents[0],
        routes[:, 0].transpose(0, 2, 1),
        route_weights[:, 0].transpose(0, 2, 1),
        w_gate[0, 0],
        w_up[0, 0],
        w_down[0, 0],
    )
    first_segment = lax.axis_index("segment") == 0
    finished = jnp.where(first_segment, backward_out, forward_out)
    handed = lax.ppermute(
        jnp.where(first_segment, forward_out, backward_out), "segment", [(0, 1), (1, 0)]
    )
    return (finished[None], handed[None])


def solution(mesh):
    placed = (
        P("segment", "expert", None),
        P("segment", "expert", None),
        P("segment", "expert", None),
        P(None, "segment", "expert", None),
        P(None, "segment", "expert", None),
        P("segment", "expert", None, None),
        P("segment", "expert", None, None),
        P("segment", "expert", None, None),
    )
    return jax.shard_map(
        per_device,
        mesh=mesh,
        in_specs=placed,
        out_specs=(P("segment", "expert", None), P("segment", "expert", None)),
        check_vma=False,
    )
```

time: 493 us -> 259 us (0.53); the launches traced: 485 us -> 259 us
  waiting for transfers between devices: 272 us -> 10.9 us
  Pallas kernels: 0 us -> 241 us
  local copies, waits for them, and re-layouts: 78.5 us -> 0.79 us
  matrix products: 70.9 us -> 0 us
  starting transfers between devices: 52.3 us -> 3.18 us
  other arithmetic: 9.51 us -> 2.07 us
    all_to_all x5 -> x0, waiting for transfers between devices: 260 us -> none  [the longest x2 107 us: per_device(): lax.all_to_all(result_rows, 'expert', split_axis=0, concat_axis=0, tiled=...]
    pallas_call x0 -> x1, Pallas kernels: none -> 241 us  [moe(): pl.pallas_call(kernel, out_shape=(jax.ShapeDtypeStruct(block, BF16), jax....]
    reshape x10 -> x0, local copies, waits for them, and re-layouts: 76.8 us -> none  [the longest x1 7.79 us: per_device(): received[1].reshape(-1, width)]
    dot_general x15 -> x0, matrix products: 70.9 us -> none  [the longest x3 18.9 us: dot_transposed(): lax.dot_general(left, right, (((1,), (1,)), ((), ())), preferred_element_...]
    all_to_all x5 -> x0, starting transfers between devices: 49.7 us -> none  [the longest x2 19.3 us: per_device(): lax.all_to_all(result_rows, 'expert', split_axis=0, concat_axis=0, tiled=...]
    reduce_sum x6 -> x0, other arithmetic: 8.8 us -> none  [the longest x1 6.55 us: slot_plan(): jnp.sum((targets[None, :, :] == slot_ids[:, None, None]).astype(jnp.float...]
  transfers between devices with their start and end apart: 6 -> 1, of which waited for: 6 -> 1; matrix products, arithmetic and copies ran while one was open for 26% -> 0% of each run, Pallas kernels for 0% -> 0%
where the time goes in v1:
time: 259 us
  Pallas kernels  241 us (93%)
  waiting for transfers between devices  10.9 us (4%)
  starting transfers between devices  3.18 us (1%)
    pallas_call x1, Pallas kernels, moe(): pl.pallas_call(kernel, out_shape=(jax.ShapeDtypeStruct(block, BF16), jax....  241 us
    ppermute x1, waiting for transfers between devices, per_device(): lax.ppermute(jnp.where(first_segment, forward_out, backward_out), 'segmen...  10.9 us
  transfers between devices with their start and end apart: 1, of which 1 were waited for; matrix products, arithmetic and copies ran while one was open for 0% of the time, Pallas kernels for 0%

profile of v1, /device:TPU:1, one launch (start us, length us, event | category | flops | bytes accessed | tf_op | source)
XLA Modules:
  0.0 258.7 jit_solution(942894144173435244)
XLA Ops:
  0.6 241.1 %shard_map.95 = (bf16[128,2048]{1,0:T(8,128)(2,1)}, bf16[128,2048]{1,0:T(8,128)(2,1)}, bf16[3,8,128,2048]{3,2,1,0:T(8,128)(2,1)}) custom-call(bf16[128,2048]{1,0:T(8,128)(2,1)} %bitcast.19, bf16[128,2048]{1,0:T(8,128)(2,1)} %bitcast.20, bf16[128,2048]{1,0:T(8,128)(2,1)} %bitcast.21, s32[2,8,128]{2,1,0:T(8,128)} %bitcast.22, f32[2,8,128]{2,1,0:T(8,128)} %bitcast.23, ...), custom_call_target="tpu_custom_call" | custom-call | tf_op jit(solution)/shard_map/pallas_call | solution.py:415
  241.8 2.1 broadcast_select_fusion
  243.9 3.2 %collective-permute-start = (bf16[128,2048]{1,0:T(8,128)(2,1)S(1)}, bf16[128,2048]{1,0:T(8,128)(2,1)S(1)}, u32[]{:S(2)}, u32[]{:S(2)}) collective-permute-start(bf16[128,2048]{1,0:T(8,128)(2,1)S(1)} %get-tuple-element.6), channel_id=1, source_target_pairs={{0,64},{64,0},{1,65},{65,1},{2,66},{66,2},{3,67},{67,3},{4,68},{68... | collective-permute-start | bytes 1572872 | tf_op jit(solution)/shard_map/ppermute | solution.py:482
  247.0 10.9 %collective-permute-done = bf16[128,2048]{1,0:T(8,128)(2,1)S(1)} collective-permute-done((bf16[128,2048]{1,0:T(8,128)(2,1)S(1)}, bf16[128,2048]{1,0:T(8,128)(2,1)S(1)}, u32[]{:S(2)}, u32[]{:S(2)}) %collective-permute-start) | collective-permute-done | bytes 524320 | tf_op jit(solution)/shard_map/ppermute | solution.py:482
  257.9 0.8 copy.11
Async XLA Ops:
  243.9 14.0 %collective-permute-start = (bf16[128,2048]{1,0:T(8,128)(2,1)S(1)}, bf16[128,2048]{1,0:T(8,128)(2,1)S(1)}, u32[]{:S(2)}, u32[]{:S(2)}) collective-permute-start(bf16[128,2048]{1,0:T(8,128)(2,1)S(1)} %get-tuple-element.6), channel_id=1, source_target_pairs={{0,64},{64,0},{1,65},{65,1},{2,66},{66,2},{3,67},{67,3},{4,68},{68... | collective-permute-start | bytes 1572872 | tf_op jit(solution)/shard_map/ppermute | solution.py:482

commit v2 on v1

v2 whole, which is shorter than its diff:
```python
import functools

import jax
import jax.numpy as jnp
from jax import lax
from jax.experimental import pallas as pl
from jax.experimental.pallas import tpu as pltpu
from jax.sharding import PartitionSpec as P

MESH = pl.DeviceIdType.MESH
F32 = jnp.float32
BF16 = jnp.bfloat16

TOK = 128
CAP = 17
SRC = 8
DST = 8
BLK = 144
TILES = BLK // 16
FAR = (2, 1, 3)
DIRECT = (32, 64, 32)
REDUCE = (96, 32)
PARTS = 2
WIDE = 2048 // PARTS
SLOTS = 4


def dot(left, right):
    return jnp.dot(left, right, preferred_element_type=F32)


def dot_nt(left, right):
    return lax.dot_general(left, right, (((1,), (1,)), ((), ())), preferred_element_type=F32)


def dot_tn(left, right):
    return lax.dot_general(left, right, (((0,), (0,)), ((), ())), preferred_element_type=F32)


def kernel(
    xf, xb, xc, routes, weights, wg_hbm, wu_hbm, wd_hbm,
    finished, handed, gathered,
    town, table, gt, packed, recv, back, crossed, f_y, f_a, acc, ready, hid, wg, wu, wd,
    w_sem, fetch_sem, loc_sem, keep_sem, oloc_sem,
    t_s, t_r, g1_s, g1_r, g2_s, g2_r, g2f_s, g2f_r, g3_s, g3_r, g3f_s, g3f_r, g4_s, g4_r, a_s, a_r, o_s, o_r,
    c1_s, c1_r, c2_s, c2_r, c3_s, c3_r, c4_s, c4_r, h_s, h_r,
):
    seg = lax.axis_index("segment")
    me = lax.axis_index("expert")
    z, y, x, c = me // 16, (me // 8) % 2, (me // 2) % 4, me % 2
    a = z * (1 - c) + x * c
    b = x * (1 - c) + z * c
    inputs = (xf, xb, xc)

    def device(aa, yy, bb, cc):
        zz = aa * (1 - c) + bb * c
        xx = bb * (1 - c) + aa * c
        return (seg, ((zz * 2 + yy) * 4 + xx) * 2 + cc)

    def at_a(d, dy=0):
        return device((a + d) % 4, (y + dy) % 2, b, c)

    def source(d, dy=0):
        return ((a + d + 4) % 4) * 2 + (y + dy) % 2

    own = a * 2 + y

    def remote(src, dst, send, rec, to):
        return pltpu.make_async_remote_copy(
            src_ref=src, dst_ref=dst, send_sem=send, recv_sem=rec, device_id=to, device_id_type=MESH
        )

    loads = [
        pltpu.make_async_copy(src, dst, w_sem.at[i])
        for i, (src, dst) in enumerate(((wg_hbm, wg), (wu_hbm, wu), (wd_hbm, wd)))
    ]

    barrier = pltpu.get_barrier_semaphore()
    partners = [at_a(d, dy) for d in range(4) for dy in range(2) if d or dy]
    partners += [device(a, y, (b + d) % 4, c) for d in (1, 2, 3)]
    partners += [device(a, y, (b + d) % 4, 1 - c) for d in range(4)]
    partners += [device((a + d) % 4, y, b, 1 - c) for d in (1, 2, 3)]
    partners += [(1 - seg, me)]
    for to in partners:
        pl.semaphore_signal(barrier, inc=1, device_id=to, device_id_type=MESH)
    pl.semaphore_wait(barrier, len(partners))

    def columns(h):
        return pl.ds(WIDE * h, WIDE)

    def g1(q, h):
        return remote(
            inputs[q].at[:, columns(h)], gathered.at[q, h, own], g1_s.at[q, h], g1_r.at[q, h], at_a(0, 1)
        )

    def g2(q, h, d):
        return remote(
            inputs[q].at[:, columns(h)], gathered.at[q, h, own], g2_s.at[q, h, d], g2_r.at[q, h, d],
            at_a(d),
        )

    def g2f(q, h, d):
        part = gathered.at[q, h, source(-d), pl.ds(0 if d == 1 else TOK // 2, TOK // 2)]
        return remote(part, part, g2f_s.at[q, h, d], g2f_r.at[q, h, d], at_a(d))

    def g3(q, h, d):
        part = gathered.at[q, h, source(0, 1), pl.ds(0, DIRECT[q])]
        return remote(part, part, g3_s.at[q, h, d], g3_r.at[q, h, d], at_a(d))

    def g3f(q, h, d):
        half = DIRECT[q] // 2
        part = gathered.at[q, h, source(-d, 1), pl.ds(0 if d == 1 else half, half)]
        return remote(part, part, g3f_s.at[q, h, d], g3f_r.at[q, h, d], at_a(d))

    def g4(q, h, d):
        part = gathered.at[q, h, source(-d), pl.ds(DIRECT[q], TOK - DIRECT[q])]
        return remote(part, part, g4_s.at[q, h, d], g4_r.at[q, h, d], at_a(0, 1))

    def fetch(q, h, d, dy):
        s = source(d, dy)
        src = inputs[q].at[:, columns(h)] if (d, dy) == (0, 0) else gathered.at[q, h, s]
        return pltpu.make_async_copy(src, gt.at[h, s], fetch_sem.at[h, 2 * d + dy])

    def gather_own(q, h):
        g1(q, h).start()
        for d in (1, 3):
            g2(q, h, d).start()

    def gather_relay(q, h):
        g1(q, h).wait_recv()
        for d in (1, 3):
            g3(q, h, d).start()
        for d in (1, 3):
            g2(q, h, d).wait_recv()
            g2f(q, h, d).start()
            g4(q, h, d).start()

    def gather_onward(q, h):
        for d in (1, 3):
            g3(q, h, d).wait_recv()
            g3f(q, h, d).start()
        for d in (1, 3):
            g2f(q, h, d).wait_recv()
        g4(q, h, 2).start()
        for dy in range(2):
            fetch(q, h, 0, dy).start()
        for d in range(1, 4):
            fetch(q, h, d, 0).start()

    def gather_rest(q, h):
        for d in (1, 3):
            g4(q, h, d).wait_recv()
            fetch(q, h, 4 - d, 1).start()
        for d in (1, 3):
            g3f(q, h, d).wait_recv()
        g4(q, h, 2).wait_recv()
        fetch(q, h, 2, 1).start()

    def gather_sent(q, h):
        g1(q, h).wait_send()
        for d in (1, 3):
            g2(q, h, d).wait_send()
            g2f(q, h, d).wait_send()
            g3(q, h, d).wait_send()
            g3f(q, h, d).wait_send()
        for d in FAR:
            g4(q, h, d).wait_send()

    units = [(q, h) for q in (1, 2, 0) for h in range(PARTS)]
    gather_own(*units[0])
    for load in loads:
        load.start()

    row = lax.broadcasted_iota(jnp.int32, (64, TOK), 0)
    ra, ry, rb, rc = row // 16, (row // 8) % 2, (row // 2) % 4, row % 2
    expert = (
        ((ra * (1 - c) + rb * c) * 2 + ry) * 4 + (rb * (1 - c) + ra * c)
    ) * 2 + rc
    before = (
        lax.broadcasted_iota(jnp.int32, (TOK, TOK), 0)
        < lax.broadcasted_iota(jnp.int32, (TOK, TOK), 1)
    ).astype(F32).astype(BF16)
    for p in range(2):
        named = jnp.zeros((64, TOK), F32)
        weight = jnp.zeros((64, TOK), F32)
        for j in range(8):
            hit = routes[p, j : j + 1, :] == expert
            named = jnp.where(hit, 1.0, named)
            weight = jnp.where(hit, weights[p, j : j + 1, :], weight)
        prior = dot(named.astype(BF16), before)
        place = jnp.where(named > 0.5, prior, -1000.0)
        for g in range(8):
            town[g, 2 * p] = place[8 * g : 8 * g + 8]
            town[g, 2 * p + 1] = weight[8 * g : 8 * g + 8]

    def send_table(d, dy):
        return remote(
            town.at[source(d, dy)], table.at[own], t_s.at[2 * d + dy], t_r.at[2 * d + dy], at_a(d, dy)
        )

    near = [(d, dy) for d in range(4) for dy in range(2) if d or dy]
    for d, dy in near:
        send_table(d, dy).start()
    table[own] = town[own]

    slot_row = lax.broadcasted_iota(jnp.int32, (DST, 16, TOK), 1).astype(F32)

    def pack(q, h, buf):
        def step(i, carry):
            s0 = jnp.clip(i - 1, 0, SRC - 2)
            parts = []
            for o in range(2):
                place = table[s0 + o, 2 * min(q, 1)]
                shift = (CAP * (s0 + o) - 16 * i).astype(F32)
                parts.append(
                    jnp.where(place[:, None, :] + shift == slot_row, 1.0, 0.0).reshape(DST * 16, TOK)
                )
            pick = jnp.concatenate(parts, axis=1).astype(BF16)
            rows = gt[h, pl.ds(s0, 2)].reshape(2 * TOK, WIDE)
            made = dot(pick, rows).astype(BF16).reshape(DST, 16, WIDE)
            packed[buf, :, pl.ds(pl.multiple_of(16 * i, 16), 16), :] = made
            return carry

        lax.fori_loop(0, TILES, step, 0)

    near_b = [(d, dc) for d in (2, 1, 3, 0) for dc in range(2) if d or dc]

    def scatter(q, h, d, dc):
        buf = units.index((q, h)) % SLOTS
        bb, cc = (b + d) % 4, (c + dc) % 2
        return remote(
            packed.at[buf, bb * 2 + cc], recv.at[q, 2 * d + dc, :, columns(h)],
            a_s.at[q, h, 2 * d + dc], a_r.at[q, h, 2 * d + dc], device(a, y, bb, cc),
        )

    def scatter_own(q, h):
        buf = units.index((q, h)) % SLOTS
        return pltpu.make_async_copy(
            packed.at[buf, b * 2 + c], recv.at[q, 0, :, columns(h)], loc_sem.at[q, h]
        )

    def scatter_sent(q, h):
        for d, dc in near_b:
            scatter(q, h, d, dc).wait_send()
        scatter_own(q, h).wait()

    def pack_and_send(q, h):
        for d in range(4):
            for dy in range(2):
                fetch(q, h, d, dy).wait()
        pack(q, h, units.index((q, h)) % SLOTS)
        for d, dc in near_b:
            scatter(q, h, d, dc).start()
        scatter_own(q, h).start()

    def scatter_wait(q, k):
        for h in range(PARTS):

            @pl.when(k > 0)
            def _():
                scatter(q, h, k, 0).wait_recv()

            scatter(q, h, k, 1).wait_recv()

    def result_same(p, h, k):
        return remote(
            recv.at[p, 2 * k, :, columns(h)], back.at[p, b * 2 + c, :, columns(h)],
            o_s.at[p, h, 2 * k], o_r.at[p, h, 2 * k], device(a, y, (b - k + 4) % 4, c),
        )

    def result_other(p, h, k):
        return remote(
            recv.at[p, 2 * k + 1, :, columns(h)], back.at[p, a * 2 + c, :, columns(h)],
            o_s.at[p, h, 2 * k + 1], o_r.at[p, h, 2 * k + 1], device((a - k + 4) % 4, y, b, 1 - c),
        )

    def result_own(p, h):
        return pltpu.make_async_copy(
            recv.at[p, 0, :, columns(h)], back.at[p, b * 2 + c, :, columns(h)], oloc_sem.at[p, h]
        )

    def send_results(p, h, k):
        @pl.when(k == 0)
        def _():
            result_own(p, h).start()

        @pl.when(k > 0)
        def _():
            result_same(p, h, k).start()

        result_other(p, h, k).start()

    def results_wait(p, h):
        result_own(p, h).wait()
        for k in range(4):
            if k:
                result_same(p, h, k).wait_recv()
            result_other(p, h, k).wait_recv()

    def results_sent(p, h):
        for k in range(4):
            if k:
                result_same(p, h, k).wait_send()
            result_other(p, h, k).wait_send()

    def forward_hidden(k):
        scatter_wait(0, k)
        rows = recv[0, pl.ds(2 * k, 2)].reshape(2 * BLK, 2048)
        for n in range(3):
            cols = slice(256 * n, 256 * n + 256)
            gate = dot(rows, wg[:, cols])
            up = dot(rows, wu[:, cols])
            hid[0, k, :, cols] = (gate * jax.nn.sigmoid(gate) * up).astype(BF16)

    def forward_part(h, k):
        for n in range(WIDE // 512):
            cols = slice(WIDE * h + 512 * n, WIDE * h + 512 * n + 512)
            recv[0, pl.ds(2 * k, 2), :, cols] = (
                dot(hid[0, k], wd[:, cols]).astype(BF16).reshape(2, BLK, 512)
            )
        send_results(0, h, k)

    def backward_hidden(k):
        scatter_wait(1, k)
        scatter_wait(2, k)
        rows = recv[1, pl.ds(2 * k, 2)].reshape(2 * BLK, 2048)
        cot = recv[2, pl.ds(2 * k, 2)].reshape(2 * BLK, 2048)
        for n in range(3):
            cols = slice(256 * n, 256 * n + 256)
            gate = dot(rows, wg[:, cols])
            up = dot(rows, wu[:, cols])
            grad = dot_nt(cot, wd[cols, :])
            sig = jax.nn.sigmoid(gate)
            hid[0, k, :, cols] = (grad * up * sig * (1.0 + gate * (1.0 - sig))).astype(BF16)
            hid[1, k, :, cols] = (grad * gate * sig).astype(BF16)

    def backward_part(h, k):
        for n in range(WIDE // 512):
            cols = slice(WIDE * h + 512 * n, WIDE * h + 512 * n + 512)
            recv[1, pl.ds(2 * k, 2), :, cols] = (
                (dot_nt(hid[0, k], wg[cols, :]) + dot_nt(hid[1, k], wu[cols, :]))
                .astype(BF16)
                .reshape(2, BLK, 512)
            )
        send_results(1, h, k)

    def loop(*steps):
        def body(k, carry):
            for step in steps:
                step(k)
            return carry

        lax.fori_loop(0, 4, body, 0)

    pair_row = lax.broadcasted_iota(jnp.int32, (DST, 32, TOK), 1).astype(F32)

    def partial(p, h, d, dy):
        s = source(d, dy)
        place = table[s, 2 * p]
        weight = table[s, 2 * p + 1]
        hit = place[:, None, :] + s.astype(F32) == pair_row
        mix = jnp.where(hit, weight[:, None, :], 0.0).reshape(DST * 32, TOK).astype(BF16)
        rows = back[p, :, pl.ds(pl.multiple_of(16 * s, 16), 32), columns(h)]
        return dot_tn(mix, rows.reshape(DST * 32, WIDE))

    sums = gt

    def c1(p, h, d):
        part = pl.ds(0, REDUCE[p])
        return remote(
            sums.at[h, 2 * d + 1, part], crossed.at[p, d - 1, part, columns(h)],
            c1_s.at[p, h, d], c1_r.at[p, h, d], at_a(d),
        )

    def c2(p, h, d):
        part = pl.ds(REDUCE[p], TOK - REDUCE[p])
        dst = crossed.at[p, d - 1, part, columns(h)] if d else f_y.at[p, part, columns(h)]
        return remote(
            sums.at[h, 2 * d + 1, part], dst, c2_s.at[p, h, d], c2_r.at[p, h, d], at_a(0, 1)
        )

    def c3(p, h):
        part = pl.ds(0, REDUCE[p])
        return remote(
            sums.at[h, 1, part], f_y.at[p, part, columns(h)], c3_s.at[p, h], c3_r.at[p, h],
            at_a(0, 1),
        )

    def c4(p, h, d):
        return remote(
            sums.at[h, 2 * d], f_a.at[p, d - 1, :, columns(h)],
            c4_s.at[p, h, d], c4_r.at[p, h, d], at_a(d),
        )

    def combine_start(p, h):
        cols = columns(h)
        results_wait(p, h)
        for d in (2, 1, 3):
            sums[h, 2 * d + 1] = partial(p, h, d, 1).astype(BF16)
            c1(p, h, d).start()
            c2(p, h, d).start()
        sums[h, 1] = partial(p, h, 0, 1).astype(BF16)
        c2(p, h, 0).start()
        for d in (2, 1, 3):
            sums[h, 2 * d] = partial(p, h, d, 0).astype(BF16)
        acc[:, cols] = partial(p, h, 0, 0) + inputs[2 * p][:, cols].astype(F32)

    def combine_middle(p, h):
        cols = columns(h)
        cut = REDUCE[p]
        for d in (2, 1, 3):
            c2(p, h, d).wait_recv()
            sums[h, 2 * d, cut:, :] = (
                sums[h, 2 * d, cut:, :].astype(F32) + crossed[p, d - 1, cut:, cols].astype(F32)
            ).astype(BF16)
            c4(p, h, d).start()
        for d in (1, 3, 2):
            c1(p, h, d).wait_recv()
        total = sums[h, 1, :cut, :].astype(F32)
        for d in (1, 2, 3):
            total += crossed[p, d - 1, :cut, cols].astype(F32)
        sums[h, 1, :cut, :] = total.astype(BF16)
        c3(p, h).start()

    def hand(p, h):
        part = ready.at[p, :, columns(h)]
        return remote(part, handed.at[:, columns(h)], h_s.at[p, h], h_r.at[p, h], (1 - seg, me))

    def keep(p, h):
        return pltpu.make_async_copy(
            ready.at[p, :, columns(h)], finished.at[:, columns(h)], keep_sem.at[h]
        )

    def combine_end(p, h):
        cols = columns(h)
        for d in (1, 3, 2):
            c4(p, h, d).wait_recv()
        c2(p, h, 0).wait_recv()
        c3(p, h).wait_recv()
        total = acc[:, cols] + f_y[p, :, cols].astype(F32)
        for d in (1, 2, 3):
            total += f_a[p, d - 1, :, cols].astype(F32)
        ready[p, :, cols] = total.astype(BF16)

        @pl.when(seg == p)
        def _():
            hand(p, h).start()

        @pl.when(seg == 1 - p)
        def _():
            keep(p, h).start()

    def combine_sent(p, h):
        for d in range(4):
            if d:
                c1(p, h, d).wait_send()
                c4(p, h, d).wait_send()
            c2(p, h, d).wait_send()
        c3(p, h).wait_send()

    def stage(step, i):
        if i < len(units):
            step(*units[i])

    stage(gather_relay, 0)
    stage(gather_own, 1)
    stage(gather_onward, 0)
    stage(gather_relay, 1)
    stage(gather_own, 2)
    for i, unit in enumerate(units):
        gather_rest(*unit)
        if i == 0:
            for d, dy in near:
                send_table(d, dy).wait_recv()
        if i >= SLOTS:
            scatter_sent(*units[i - SLOTS])
        pack_and_send(*unit)
        stage(gather_onward, i + 1)
        stage(gather_relay, i + 2)
        stage(gather_own, i + 3)
    for load in loads:
        load.wait()
    for unit in units[-SLOTS:]:
        scatter_own(*unit).wait()
    loop(backward_hidden, functools.partial(backward_part, 0))
    for h in range(1, PARTS):
        loop(functools.partial(backward_part, h))
    for h in range(PARTS):
        combine_start(1, h)
    loop(forward_hidden, functools.partial(forward_part, 0))
    for h in range(PARTS):
        combine_middle(1, h)
    for h in range(1, PARTS):
        loop(functools.partial(forward_part, h))
    for h in range(PARTS):
        combine_end(1, h)
    for h in range(PARTS):
        combine_sent(1, h)
    for h in range(PARTS):
        combine_start(0, h)
        if h:
            combine_middle(0, h - 1)
    combine_middle(0, PARTS - 1)
    for h in range(PARTS):
        combine_end(0, h)
    for h in range(PARTS):
        combine_sent(0, h)

    for p in range(2):
        for h in range(PARTS):
            results_sent(p, h)

            @pl.when(seg == p)
            def _():
                hand(p, h).wait_send()

            @pl.when(seg == 1 - p)
            def _():
                keep(p, h).wait()
                hand(p, h).wait_recv()

    for d, dy in near:
        send_table(d, dy).wait_send()
    for q, h in units:
        gather_sent(q, h)
    for q, h in units[-SLOTS:]:
        for d, dc in near_b:
            scatter(q, h, d, dc).wait_send()


def moe(xf, xb, xc, routes, weights, wg, wu, wd):
    vmem = pl.BlockSpec(memory_space=pltpu.VMEM)
    hbm = pl.BlockSpec(memory_space=pl.ANY)
    dma = pltpu.SemaphoreType.DMA
    block = (TOK, 2048)
    finished, handed, _ = pl.pallas_call(
        kernel,
        out_shape=(
            jax.ShapeDtypeStruct(block, BF16),
            jax.ShapeDtypeStruct(block, BF16),
            jax.ShapeDtypeStruct((3, PARTS, SRC, TOK, WIDE), BF16),
        ),
        in_specs=[vmem] * 5 + [hbm] * 3,
        out_specs=(hbm, hbm, hbm),
        scratch_shapes=[
            pltpu.VMEM((8, 4, 8, TOK), F32),
            pltpu.VMEM((8, 4, 8, TOK), F32),
            pltpu.VMEM((PARTS, SRC, TOK, WIDE), BF16),
            pltpu.VMEM((SLOTS, DST, BLK, WIDE), BF16),
            pltpu.VMEM((3, 8, BLK, 2048), BF16),
            pltpu.VMEM((2, DST, BLK, 2048), BF16),
            pltpu.VMEM((2, 3) + block, BF16),
            pltpu.VMEM((2,) + block, BF16),
            pltpu.VMEM((2, 3) + block, BF16),
            pltpu.VMEM(block, F32),
            pltpu.VMEM((2,) + block, BF16),
            pltpu.VMEM((2, 4, 2 * BLK, 768), BF16),
            pltpu.VMEM((2048, 768), BF16),
            pltpu.VMEM((2048, 768), BF16),
            pltpu.VMEM((768, 2048), BF16),
            dma((3,)), dma((PARTS, 8)), dma((3, PARTS)), dma((PARTS,)), dma((2, PARTS)),
            dma((8,)), dma((8,)),
            dma((3, PARTS)), dma((3, PARTS)),
            dma((3, PARTS, 4)), dma((3, PARTS, 4)),
            dma((3, PARTS, 4)), dma((3, PARTS, 4)),
            dma((3, PARTS, 4)), dma((3, PARTS, 4)),
            dma((3, PARTS, 4)), dma((3, PARTS, 4)),
            dma((3, PARTS, 4)), dma((3, PARTS, 4)),
            dma((3, PARTS, 8)), dma((3, PARTS, 8)),
            dma((2, PARTS, 8)), dma((2, PARTS, 8)),
            dma((2, PARTS, 4)), dma((2, PARTS, 4)),
            dma((2, PARTS, 4)), dma((2, PARTS, 4)),
            dma((2, PARTS)), dma((2, PARTS)),
            dma((2, PARTS, 4)), dma((2, PARTS, 4)),
            dma((2, PARTS)), dma((2, PARTS)),
        ],
        compiler_params=pltpu.CompilerParams(
            collective_id=0, has_side_effects=True, vmem_limit_bytes=63 * 2**20
        ),
    )(xf, xb, xc, routes, weights, wg, wu, wd)
    return finished, handed


def per_device(
    forward_inputs,
    backward_inputs,
    backward_cotangents,
    routes,
    route_weights,
    w_gate,
    w_up,
    w_down,
):
    finished, handed = moe(
        forward_inputs[0],
        backward_inputs[0],
        backward_cotangents[0],
        routes[:, 0].transpose(0, 2, 1),
        route_weights[:, 0].transpose(0, 2, 1),
        w_gate[0, 0],
        w_up[0, 0],
        w_down[0, 0],
    )
    return (finished[None], handed[None])


def solution(mesh):
    placed = (
        P("segment", "expert", None),
        P("segment", "expert", None),
        P("segment", "expert", None),
        P(None, "segment", "expert", None),
        P(None, "segment", "expert", None),
        P("segment", "expert", None, None),
        P("segment", "expert", None, None),
        P("segment", "expert", None, None),
    )
    return jax.shard_map(
        per_device,
        mesh=mesh,
        in_specs=placed,
        out_specs=(P("segment", "expert", None), P("segment", "expert", None)),
        check_vma=False,
    )
```

time: 259 us -> 245 us (0.946)
  waiting for transfers between devices: 10.9 us -> 0 us
  starting transfers between devices: 3.18 us -> 0 us
  local copies, waits for them, and re-layouts: 0.79 us -> 3.76 us
    ppermute x1 -> x0, waiting for transfers between devices: 10.9 us -> none  [per_device(): lax.ppermute(jnp.where(first_segment, forward_out, backward_out), 'segmen...]
    ppermute x1 -> x0, starting transfers between devices: 3.18 us -> none  [per_device(): lax.ppermute(jnp.where(first_segment, forward_out, backward_out), 'segmen...]
    unnamed x1 -> x2, local copies, waits for them, and re-layouts: 0.79 us -> 3.76 us
  transfers between devices with their start and end apart: 1 -> 0, of which waited for: 1 -> 0; matrix products, arithmetic and copies ran while one was open for 0% -> 0% of each run, Pallas kernels for 0% -> 0%
where the time goes in v2:
time: 245 us; the launch traced here: 244 us
  Pallas kernels  240 us (98%)
  local copies, waits for them, and re-layouts  3.76 us (2%)
    pallas_call x1, Pallas kernels, moe(): pl.pallas_call(kernel, out_shape=(jax.ShapeDtypeStruct(block, BF16), jax....  240 us

profile of v2, /device:TPU:1, one launch (start us, length us, event | category | flops | bytes accessed | tf_op | source)
XLA Modules:
  0.0 244.1 jit_solution(14478568984416695876)
XLA Ops:
  0.6 239.7 %shard_map.95 = (bf16[128,2048]{1,0:T(8,128)(2,1)}, bf16[128,2048]{1,0:T(8,128)(2,1)}, bf16[3,2,8,128,1024]{4,3,2,1,0:T(8,128)(2,1)}) custom-call(bf16[128,2048]{1,0:T(8,128)(2,1)} %bitcast.19, bf16[128,2048]{1,0:T(8,128)(2,1)} %bitcast.20, bf16[128,2048]{1,0:T(8,128)(2,1)} %bitcast.21, s32[2,8,128]{2,1,0:T(8,128)} %bitcast.22, f32[2,8,128]{2,1,0:T(8,128)} %bitcast.23, ...), custom_call_target="tpu_custom_call" | custom-call | tf_op jit(solution)/shard_map/pallas_call | solution.py:536
  240.3 1.9 copy.12
  242.2 1.9 copy.13

commit v3 on v2

--- a/solution.py
+++ b/solution.py
@@ -18,8 +18,8 @@
 BLK = 144
 TILES = BLK // 16
 FAR = (2, 1, 3)
-DIRECT = (32, 64, 32)
-REDUCE = (96, 32)
+DIRECT = (32, 96, 32)
+REDUCE = (96, 16)
 PARTS = 2
 WIDE = 2048 // PARTS
 SLOTS = 4
@@ -41,7 +41,7 @@
     xf, xb, xc, routes, weights, wg_hbm, wu_hbm, wd_hbm,
     finished, handed, gathered,
     town, table, gt, packed, recv, back, crossed, f_y, f_a, acc, ready, hid, wg, wu, wd,
-    w_sem, fetch_sem, loc_sem, keep_sem, oloc_sem,
+    w_sem, fetch_sem, loc_sem, oloc_sem,
     t_s, t_r, g1_s, g1_r, g2_s, g2_r, g2f_s, g2f_r, g3_s, g3_r, g3f_s, g3f_r, g4_s, g4_r, a_s, a_r, o_s, o_r,
     c1_s, c1_r, c2_s, c2_r, c3_s, c3_r, c4_s, c4_r, h_s, h_r,
 ):
@@ -223,7 +223,7 @@
 
         lax.fori_loop(0, TILES, step, 0)
 
-    near_b = [(d, dc) for d in (2, 1, 3, 0) for dc in range(2) if d or dc]
+    near_b = [(d, dc) for d in (1, 3, 2, 0) for dc in range(2) if d or dc]
 
     def scatter(q, h, d, dc):
         buf = units.index((q, h)) % SLOTS
@@ -395,20 +395,20 @@
     def combine_start(p, h):
         cols = columns(h)
         results_wait(p, h)
-        for d in (2, 1, 3):
+        for d in (1, 3, 2):
             sums[h, 2 * d + 1] = partial(p, h, d, 1).astype(BF16)
             c1(p, h, d).start()
             c2(p, h, d).start()
         sums[h, 1] = partial(p, h, 0, 1).astype(BF16)
         c2(p, h, 0).start()
-        for d in (2, 1, 3):
+        for d in (1, 3, 2):
             sums[h, 2 * d] = partial(p, h, d, 0).astype(BF16)
         acc[:, cols] = partial(p, h, 0, 0) + inputs[2 * p][:, cols].astype(F32)
 
     def combine_middle(p, h):
         cols = columns(h)
         cut = REDUCE[p]
-        for d in (2, 1, 3):
+        for d in (1, 3, 2):
             c2(p, h, d).wait_recv()
             sums[h, 2 * d, cut:, :] = (
                 sums[h, 2 * d, cut:, :].astype(F32) + crossed[p, d - 1, cut:, cols].astype(F32)
@@ -423,13 +423,8 @@
         c3(p, h).start()
 
     def hand(p, h):
-        part = ready.at[p, :, columns(h)]
+        part = ready.at[:, columns(h)]
         return remote(part, handed.at[:, columns(h)], h_s.at[p, h], h_r.at[p, h], (1 - seg, me))
-
-    def keep(p, h):
-        return pltpu.make_async_copy(
-            ready.at[p, :, columns(h)], finished.at[:, columns(h)], keep_sem.at[h]
-        )
 
     def combine_end(p, h):
         cols = columns(h)
@@ -440,15 +435,15 @@
         total = acc[:, cols] + f_y[p, :, cols].astype(F32)
         for d in (1, 2, 3):
             total += f_a[p, d - 1, :, cols].astype(F32)
-        ready[p, :, cols] = total.astype(BF16)
 
         @pl.when(seg == p)
         def _():
+            ready[:, cols] = total.astype(BF16)
             hand(p, h).start()
 
         @pl.when(seg == 1 - p)
         def _():
-            keep(p, h).start()
+            finished[:, cols] = total.astype(BF16)
 
     def combine_sent(p, h):
         for d in range(4):
@@ -485,22 +480,18 @@
     loop(backward_hidden, functools.partial(backward_part, 0))
     for h in range(1, PARTS):
         loop(functools.partial(backward_part, h))
-    for h in range(PARTS):
-        combine_start(1, h)
+    combine_start(1, 0)
     loop(forward_hidden, functools.partial(forward_part, 0))
-    for h in range(PARTS):
-        combine_middle(1, h)
-    for h in range(1, PARTS):
-        loop(functools.partial(forward_part, h))
+    combine_start(1, 1)
+    combine_middle(1, 0)
+    loop(functools.partial(forward_part, 1))
+    combine_middle(1, 1)
     for h in range(PARTS):
         combine_end(1, h)
+        combine_sent(1, h)
+        combine_start(0, h)
     for h in range(PARTS):
-        combine_sent(1, h)
-    for h in range(PARTS):
-        combine_start(0, h)
-        if h:
-            combine_middle(0, h - 1)
-    combine_middle(0, PARTS - 1)
+        combine_middle(0, h)
     for h in range(PARTS):
         combine_end(0, h)
     for h in range(PARTS):
@@ -516,7 +507,6 @@
 
             @pl.when(seg == 1 - p)
             def _():
-                keep(p, h).wait()
                 hand(p, h).wait_recv()
 
     for d, dy in near:
@@ -541,7 +531,7 @@
             jax.ShapeDtypeStruct((3, PARTS, SRC, TOK, WIDE), BF16),
         ),
         in_specs=[vmem] * 5 + [hbm] * 3,
-        out_specs=(hbm, hbm, hbm),
+        out_specs=(vmem, vmem, hbm),
         scratch_shapes=[
             pltpu.VMEM((8, 4, 8, TOK), F32),
             pltpu.VMEM((8, 4, 8, TOK), F32),
@@ -553,12 +543,12 @@
             pltpu.VMEM((2,) + block, BF16),
             pltpu.VMEM((2, 3) + block, BF16),
             pltpu.VMEM(block, F32),
-            pltpu.VMEM((2,) + block, BF16),
+            pltpu.VMEM(block, BF16),
             pltpu.VMEM((2, 4, 2 * BLK, 768), BF16),
             pltpu.VMEM((2048, 768), BF16),
             pltpu.VMEM((2048, 768), BF16),
             pltpu.VMEM((768, 2048), BF16),
-            dma((3,)), dma((PARTS, 8)), dma((3, PARTS)), dma((PARTS,)), dma((2, PARTS)),
+            dma((3,)), dma((PARTS, 8)), dma((3, PARTS)), dma((2, PARTS)),
             dma((8,)), dma((8,)),
             dma((3, PARTS)), dma((3, PARTS)),
             dma((3, PARTS, 4)), dma((3, PARTS, 4)),

time: 245 us -> 236 us (0.963)
  Pallas kernels: 240 us -> 231 us
    pallas_call x1, Pallas kernels: 240 us -> 231 us  [moe(): pl.pallas_call(kernel, out_shape=(jax.ShapeDtypeStruct(block, BF16), jax....]
where the time goes in v3:
time: 236 us
  Pallas kernels  231 us (98%)
  local copies, waits for them, and re-layouts  3.76 us (2%)
    pallas_call x1, Pallas kernels, moe(): pl.pallas_call(kernel, out_shape=(jax.ShapeDtypeStruct(block, BF16), jax....  231 us

profile of v3, /device:TPU:1, one launch (start us, length us, event | category | flops | bytes accessed | tf_op | source)
XLA Modules:
  0.0 235.9 jit_solution(3910039178603023813)
XLA Ops:
  0.6 231.5 %shard_map.95 = (bf16[128,2048]{1,0:T(8,128)(2,1)}, bf16[128,2048]{1,0:T(8,128)(2,1)}, bf16[3,2,8,128,1024]{4,3,2,1,0:T(8,128)(2,1)}) custom-call(bf16[128,2048]{1,0:T(8,128)(2,1)} %bitcast.19, bf16[128,2048]{1,0:T(8,128)(2,1)} %bitcast.20, bf16[128,2048]{1,0:T(8,128)(2,1)} %bitcast.21, s32[2,8,128]{2,1,0:T(8,128)} %bitcast.22, f32[2,8,128]{2,1,0:T(8,128)} %bitcast.23, ...), custom_call_target="tpu_custom_call" | custom-call | tf_op jit(solution)/shard_map/pallas_call | solution.py:526
  232.1 1.9 copy.12
  234.0 1.9 copy.13

commit v4 on v3

--- a/solution.py
+++ b/solution.py
@@ -223,7 +223,7 @@
 
         lax.fori_loop(0, TILES, step, 0)
 
-    near_b = [(d, dc) for d in (1, 3, 2, 0) for dc in range(2) if d or dc]
+    near_b = [(d, dc) for d in (0, 1, 3, 2) for dc in range(2) if d or dc]
 
     def scatter(q, h, d, dc):
         buf = units.index((q, h)) % SLOTS

time: 236 us -> 236 us (level)
  no operation moved by 1% of the time
where the time goes in v4:
time: 236 us
  Pallas kernels  231 us (98%)
  local copies, waits for them, and re-layouts  3.76 us (2%)
    pallas_call x1, Pallas kernels, moe(): pl.pallas_call(kernel, out_shape=(jax.ShapeDtypeStruct(block, BF16), jax....  231 us

profile of v4, /device:TPU:1, one launch (start us, length us, event | category | flops | bytes accessed | tf_op | source)
XLA Modules:
  0.0 235.8 jit_solution(15801950229216966616)
XLA Ops:
  0.6 231.4 %shard_map.95 = (bf16[128,2048]{1,0:T(8,128)(2,1)}, bf16[128,2048]{1,0:T(8,128)(2,1)}, bf16[3,2,8,128,1024]{4,3,2,1,0:T(8,128)(2,1)}) custom-call(bf16[128,2048]{1,0:T(8,128)(2,1)} %bitcast.19, bf16[128,2048]{1,0:T(8,128)(2,1)} %bitcast.20, bf16[128,2048]{1,0:T(8,128)(2,1)} %bitcast.21, s32[2,8,128]{2,1,0:T(8,128)} %bitcast.22, f32[2,8,128]{2,1,0:T(8,128)} %bitcast.23, ...), custom_call_target="tpu_custom_call" | custom-call | tf_op jit(solution)/shard_map/pallas_call | solution.py:526
  232.1 1.9 copy.12
  234.0 1.9 copy.13
